TPU v7x, 32 devices: a whole 2x2x4 slice. The times are simulated.
32 devices in a mesh: layer: 4 (over z), panel: 8 (over y, x, core).
Axes of the slice: x: 2, y: 2, z: 4, core: 2. Of those that a mesh axis runs over, the one named last changes fastest.
Arguments:
- reflections: float32 [32, 1024, 1024], P(None, 'panel'), may hold values from -0.95 to 0.95
- wave_decay: float32 [32, 1024], replicated, may hold values from 0.3 to 3
- thickness: float32 [4], P('layer'), may hold values from 0.4 to 1
- material: int32 [4], P('layer'), may hold values from 0 to 31
Outputs:
- stack_blocks: float32 [4, 1024, 1024], P('layer', 'panel')
All inputs are finite; a program needn't handle non-finite values.
Results may differ from a plain program's by a relative error of at most 0.00014.
Values sent between devices are 32-bit elements; how exact they have to be, the bound alone decides.
A program may use at most 128 MiB of HBM per device.

v0:
```python
import functools

import jax
import jax.numpy as jnp
from jax import lax
from jax.experimental import pallas as pl
from jax.experimental.pallas import tpu as pltpu
from jax.sharding import PartitionSpec as P

TERMS = 6
TILE = 256
MESH = pl.DeviceIdType.MESH


def kernel(
    n, rows, order,
    refl_ref, decay_ref, own_decay_ref, out_ref,
    land_f, land_ra, land_rb, land_ta, land_h1, land_h2, land_l,
    whi, wlo, lhs, now, mid, acc, t_other, start1, out1, out2,
    send_sem, recv_sem, zsend, zrecv,
):
    layer = lax.axis_index("layer")
    me = lax.axis_index("panel")
    half = rows // 2
    core_bit = 1
    chip_bits = [1 << i for i in range(1, n.bit_length() - 1)]
    inner = (layer == 1) | (layer == 2)
    outer = (layer == 0) | (layer == 3)

    def moved(mask):
        place = me
        bit = 1
        while bit < n:
            if mask & bit:
                place = place + bit * (1 - 2 * (me // bit % 2))
            bit *= 2
        return place

    barrier = pltpu.get_barrier_semaphore()
    for bit in chip_bits + [core_bit]:
        pl.semaphore_signal(barrier, inc=1, device_id=(layer, moved(bit)), device_id_type=MESH)
    for step in range(1, 4):
        pl.semaphore_signal(
            barrier, inc=1, device_id=((layer + step) % 4, me), device_id_type=MESH
        )
    pl.semaphore_wait(barrier, len(chip_bits) + 1 + 3)

    class Gather:
        def __init__(self, index, land, slot):
            self.index, self.land, self.slot = index, land, slot
            self.orders = [
                chip_bits + [core_bit],
                chip_bits[1:] + chip_bits[:1] + [core_bit],
            ]

        def copy(self, h, mask, bit):
            block = self.land.at[moved(mask), pl.ds(h * half, half)]
            return pltpu.make_async_remote_copy(
                src_ref=block,
                dst_ref=block,
                send_sem=send_sem.at[self.index, h, mask ^ bit],
                recv_sem=recv_sem.at[self.index, h, mask ^ bit],
                device_id=(layer, moved(bit)),
                device_id_type=MESH,
            )

        def later(self, h, mask):
            order_h = self.orders[h]
            last = max([i for i, b in enumerate(order_h) if mask & b], default=-1)
            return order_h[last + 1:]

        def start(self):
            for k in range(len(self.orders[0])):
                for h in range(2):
                    self.copy(h, 0, self.orders[h][k]).start()

        def convert(self, h, mask):
            place = moved(mask)
            block = self.land[place, h * half:(h + 1) * half]
            high = block.astype(jnp.bfloat16)
            where = pl.ds(pl.multiple_of(place * rows + h * half, half), half)
            whi[self.slot, where] = high
            wlo[self.slot, where] = (block - high.astype(jnp.float32)).astype(jnp.bfloat16)

        def masks(self):
            found = []
            for k in range(len(self.orders[0])):
                for low in range(1 << k):
                    for h in range(2):
                        mask = self.orders[h][k]
                        for i in range(k):
                            if low >> i & 1:
                                mask |= self.orders[h][i]
                        found.append((h, mask))
            return found

        def arrive(self, h, mask):
            block = self.land.at[moved(mask), pl.ds(h * half, half)]
            pltpu.make_async_remote_copy(
                src_ref=block,
                dst_ref=block,
                send_sem=send_sem.at[self.index, h, mask],
                recv_sem=recv_sem.at[self.index, h, mask],
                device_id=(layer, moved(core_bit)),
                device_id_type=MESH,
            ).wait_recv()
            for bit in self.later(h, mask):
                self.copy(h, mask, bit).start()

        def relay(self):
            for h, mask in self.masks():
                if len(self.later(h, mask)) > 1:
                    self.arrive(h, mask)

        def finish(self):
            for h in range(2):
                self.convert(h, 0)
            for h, mask in self.masks():
                if len(self.later(h, mask)) <= 1:
                    self.arrive(h, mask)
                self.convert(h, mask)

        def sent(self):
            for h, mask in self.masks():
                order_h = self.orders[h]
                bit = [b for b in order_h if mask & b][-1]
                self.copy(h, mask ^ bit, bit).wait_send()

    def zcopy(src, dst, send, recv, to):
        return pltpu.make_async_remote_copy(
            src_ref=src,
            dst_ref=dst,
            send_sem=zsend.at[send],
            recv_sem=zrecv.at[recv],
            device_id=(to, me),
            device_id_type=MESH,
        )

    def put(m, value):
        high = value.astype(jnp.bfloat16)
        lhs[0:m] = high
        lhs[m:2 * m] = (value - high.astype(jnp.float32)).astype(jnp.bfloat16)

    def multiply(m, slot, dst):
        @pl.loop(0, order // TILE)
        def _(t):
            cols = pl.ds(pl.multiple_of(t * TILE, TILE), TILE)
            large = jnp.dot(lhs[0:2 * m], whi[slot, :, cols], preferred_element_type=jnp.float32)
            small = jnp.dot(lhs[0:m], wlo[slot, :, cols], preferred_element_type=jnp.float32)
            dst[0:m, cols] = large[0:m] + large[m:2 * m] + small

    g_f = Gather(0, land_f, 0)
    g_ra = Gather(1, land_ra, 1)
    g_rb = Gather(2, land_rb, 2)
    g_ta = Gather(3, land_ta, 0)
    g_h1 = Gather(4, land_h1, 1)
    g_h2 = Gather(5, land_h2, 2)
    g_l = Gather(6, land_l, 0)

    land_f[me] = refl_ref[...]
    g_f.start()
    decays = decay_ref[...]
    now[0:rows] = own_decay_ref[...] * refl_ref[...]
    row_ids = me * rows + lax.broadcasted_iota(jnp.int32, (rows, order), 0)
    col_ids = lax.broadcasted_iota(jnp.int32, (rows, order), 1)
    acc[0:rows] = jnp.where(row_ids == col_ids, 1.0, 0.0).astype(jnp.float32)
    acc[rows:2 * rows] = now[0:rows]
    g_f.relay()
    g_f.finish()

    @pl.loop(0, TERMS - 1)
    def _(_k):
        put(rows, now[0:rows] * decay_ref[...])
        multiply(rows, 0, now)
        acc[0:rows] += now[0:rows]
        put(rows, now[0:rows] * decay_ref[...])
        multiply(rows, 0, now)
        acc[rows:2 * rows] += now[0:rows]

    put(2 * rows, acc[...])
    multiply(2 * rows, 0, mid)
    land_ra[me] = acc[rows:2 * rows] * decays - mid[0:rows]
    land_ta[me] = acc[0:rows] * decays - mid[rows:2 * rows]

    partner = layer + 1 - 2 * (layer % 2)
    r_across = zcopy(land_ra.at[me], land_rb.at[me], 0, 0, partner)
    t_across = zcopy(land_ta.at[me], t_other, 1, 1, partner)
    r_across.start()
    g_ra.start()
    g_ra.relay()
    r_across.wait_recv()
    t_across.start()
    g_rb.start()
    g_ra.finish()
    g_rb.relay()
    g_ta.start()
    g_rb.finish()
    put(rows, land_ta[me])
    multiply(rows, 2, now)
    t_across.wait_recv()
    now[rows:2 * rows] = t_other[...]
    acc[...] = now[...]

    def first_chain(_k):
        put(2 * rows, now[...])
        multiply(2 * rows, 1, mid)
        put(2 * rows, mid[...])
        multiply(2 * rows, 2, now)
        acc[...] += now[...]

    pl.loop(0, 2)(first_chain)
    g_ta.relay()
    pl.loop(2, TERMS - 1)(first_chain)
    g_ta.finish()
    put(2 * rows, acc[...])
    multiply(2 * rows, 0, mid)
    out1[...] = land_ra[me] + mid[0:rows]
    out2[...] = mid[rows:2 * rows]

    beside = layer * 3 - 3
    other = 3 - layer
    to_last = 2 - layer // 3
    h1_near = zcopy(out1, land_h1.at[me], 2, 2, beside)
    h2_across = zcopy(out1, land_h2.at[me], 3, 3, other)
    s_near = zcopy(out2, start1, 4, 4, beside)
    l_far = zcopy(out2, land_l.at[me], 5, 5, to_last)
    h2_on = zcopy(land_h2.at[me], land_h2.at[me], 6, 3, beside)
    h1_in = zcopy(land_h1.at[me], land_h1.at[me], 2, 2, other)
    h2_in = zcopy(land_h2.at[me], land_h2.at[me], 3, 3, other)
    s_in = zcopy(start1, start1, 4, 4, other)
    l_in = zcopy(land_l.at[me], land_l.at[me], 5, 5, other)

    @pl.when(inner)
    def _():
        h1_near.start()
        h2_across.start()
        land_h1[me] = out1[...]
        now[0:rows] = out2[...]

    @pl.when(outer)
    def _():
        land_l[me] = out2[...]
        h1_in.wait_recv()
        l_far.start()

    g_h1.start()
    g_h1.relay()
    h2_in.wait_recv()

    @pl.when(inner)
    def _():
        h2_on.start()
        s_near.start()

    g_h2.start()
    g_h1.finish()
    g_h2.relay()

    @pl.when(inner)
    def _():
        l_in.wait_recv()

    g_l.start()
    g_h2.finish()

    @pl.when(outer)
    def _():
        s_in.wait_recv()
        now[0:rows] = start1[...]

    acc[0:rows] = now[0:rows]

    def second_chain(_k):
        put(rows, now[0:rows])
        multiply(rows, 2, mid)
        put(rows, mid[0:rows])
        multiply(rows, 1, now)
        acc[0:rows] += now[0:rows]

    pl.loop(0, 3)(second_chain)
    g_l.relay()
    pl.loop(3, TERMS - 1)(second_chain)

    @pl.when(outer)
    def _():
        put(rows, acc[0:rows])
        multiply(rows, 2, acc)

    g_l.finish()
    put(rows, acc[0:rows])
    multiply(rows, 0, mid)

    @pl.when(inner)
    def _():
        out_ref[0] = mid[0:rows]

    @pl.when(outer)
    def _():
        out_ref[0] = mid[0:rows] + out1[...]

    for gather in (g_f, g_ra, g_rb, g_ta, g_h1, g_h2, g_l):
        gather.sent()
    r_across.wait_send()
    t_across.wait_send()

    @pl.when(inner)
    def _():
        for copy in (h1_near, h2_across, s_near, h2_on):
            copy.wait_send()

    @pl.when(outer)
    def _():
        l_far.wait_send()


def local(n, reflections, wave_decay, thickness, material):
    rows, order = reflections.shape[1:]
    me = lax.axis_index("panel")
    chosen = material[0]
    refl_rows = lax.dynamic_index_in_dim(reflections, chosen, 0, keepdims=False)
    decays = jnp.exp(
        -lax.dynamic_index_in_dim(wave_decay, chosen, 0, keepdims=False) * thickness[0]
    )
    own_decays = lax.dynamic_slice_in_dim(decays, me * rows, rows)
    whole = pltpu.VMEM((n, rows, order), jnp.float32)
    pair = pltpu.VMEM((2 * rows, order), jnp.float32)
    one = pltpu.VMEM((rows, order), jnp.float32)
    factors = pltpu.VMEM((3, order, order), jnp.bfloat16)
    return pl.pallas_call(
        functools.partial(kernel, n, rows, order),
        out_shape=jax.ShapeDtypeStruct((1, rows, order), jnp.float32),
        in_specs=[pl.BlockSpec(memory_space=pltpu.VMEM)] * 3,
        out_specs=pl.BlockSpec(memory_space=pltpu.VMEM),
        scratch_shapes=[whole] * 7 + [factors] * 2
        + [pltpu.VMEM((4 * rows, order), jnp.bfloat16)]
        + [pair] * 3 + [one] * 4
        + [pltpu.SemaphoreType.DMA((7, 2, n))] * 2
        + [pltpu.SemaphoreType.DMA((7,))] * 2,
        compiler_params=pltpu.CompilerParams(
            collective_id=0, has_side_effects=True, vmem_limit_bytes=58 * 2**20
        ),
    )(refl_rows, decays[None, :], own_decays[:, None])


def solution(mesh):
    placed = (P(None, "panel", None), P(), P("layer"), P("layer"))
    return jax.shard_map(
        functools.partial(local, mesh.shape["panel"]),
        mesh=mesh, in_specs=placed, out_specs=P("layer", "panel", None), check_vma=False,
    )
```

profile of v0, /device:TPU:0, one launch (start us, length us, event | category | flops | bytes accessed | tf_op | source)
XLA Modules:
  0.0 197.9 jit_solution(2960625879889655183)
XLA Ops:
  1.3 0.8 multiply_exponential_fusion.decay_ref
  2.1 0.0 copy-start
  2.1 0.8 copy.5.own_decay_ref
  2.9 1.9 dynamic-slice_bitcast_fusion.refl_ref
  4.7 0.0 copy-done
  4.7 191.3 %shard_map.46 = f32[1,128,1024]{2,1,0:T(8,128)} custom-call(f32[128,1024]{1,0:T(8,128)} %dynamic-slice_bitcast_fusion.refl_ref, f32[1,1024]{1,0:T(1,128)} %copy-done, f32[128,1]{1,0:T(8,128)} %copy.5.own_decay_ref), custom_call_target="tpu_custom_call" | custom-call | tf_op jit(solution)/shard_map/pallas_call | solution.py:329
  196.0 1.9 copy.9
  (1 shorter events, 0.0 us)
Async XLA Ops:
  2.1 2.7 %copy-start = (f32[1,1024]{1,0:T(1,128)}, f32[1,1024]{1,0:T(1,128)S(1)}, u32[]{:S(2)}) copy-start(f32[1,1024]{1,0:T(1,128)S(1)} %multiply_exponential_fusion.decay_ref) | copy-start | bytes 12292
where the time goes:
time: 198 us
  Pallas kernels  191 us (96%)
  local copies, waits for them, and re-layouts  4.53 us (2%)
    pallas_call x1, Pallas kernels, local(): pl.pallas_call(functools.partial(kernel, n, rows, order), out_shape=jax.S...  191 us

commit v1 on v0

--- a/solution.py
+++ b/solution.py
@@ -69,9 +69,9 @@
             last = max([i for i, b in enumerate(order_h) if mask & b], default=-1)
             return order_h[last + 1:]
 
-        def start(self):
+        def start(self, halves=(0, 1)):
             for k in range(len(self.orders[0])):
-                for h in range(2):
+                for h in halves:
                     self.copy(h, 0, self.orders[h][k]).start()
 
         def convert(self, h, mask):
@@ -136,18 +136,43 @@
             device_id_type=MESH,
         )
 
-    def put(m, value):
+    def split(buffer, m, cols, value):
         high = value.astype(jnp.bfloat16)
-        lhs[0:m] = high
-        lhs[m:2 * m] = (value - high.astype(jnp.float32)).astype(jnp.bfloat16)
-
-    def multiply(m, slot, dst):
-        @pl.loop(0, order // TILE)
-        def _(t):
-            cols = pl.ds(pl.multiple_of(t * TILE, TILE), TILE)
-            large = jnp.dot(lhs[0:2 * m], whi[slot, :, cols], preferred_element_type=jnp.float32)
-            small = jnp.dot(lhs[0:m], wlo[slot, :, cols], preferred_element_type=jnp.float32)
-            dst[0:m, cols] = large[0:m] + large[m:2 * m] + small
+        lhs[buffer, 0:m, cols] = high
+        lhs[buffer, m:2 * m, cols] = (value - high.astype(jnp.float32)).astype(jnp.bfloat16)
+
+    def put(buffer, m, value):
+        split(buffer, m, slice(None), value)
+
+    def multiply(m, slot, buffer, emit):
+        for t in range(order // TILE):
+            cols = slice(t * TILE, (t + 1) * TILE)
+            large = jnp.dot(
+                lhs[buffer, 0:2 * m], whi[slot, :, cols], preferred_element_type=jnp.float32
+            )
+            small = jnp.dot(
+                lhs[buffer, 0:m], wlo[slot, :, cols], preferred_element_type=jnp.float32
+            )
+            emit(cols, large[0:m] + large[m:2 * m] + small)
+
+    def store(dst, m):
+        def emit(cols, value):
+            dst[0:m, cols] = value
+
+        return emit
+
+    def powers(m, first, second, relay_at, relay):
+        put(0, m, acc[0:m])
+
+        def after_second(cols, value):
+            acc[0:m, cols] += value
+            split(0, m, cols, value)
+
+        @pl.loop(0, TERMS - 1)
+        def _(k):
+            multiply(m, first, 0, functools.partial(split, 1, m))
+            multiply(m, second, 1, after_second)
+            pl.when(k == relay_at)(relay)
 
     g_f = Gather(0, land_f, 0)
     g_ra = Gather(1, land_ra, 1)
@@ -168,17 +193,22 @@
     g_f.relay()
     g_f.finish()
 
+    put(0, rows, now[0:rows] * decays)
+
+    def after_layer(at, buffer):
+        def emit(cols, value):
+            acc[at:at + rows, cols] += value
+            split(buffer, rows, cols, value * decay_ref[:, cols])
+
+        return emit
+
     @pl.loop(0, TERMS - 1)
     def _(_k):
-        put(rows, now[0:rows] * decay_ref[...])
-        multiply(rows, 0, now)
-        acc[0:rows] += now[0:rows]
-        put(rows, now[0:rows] * decay_ref[...])
-        multiply(rows, 0, now)
-        acc[rows:2 * rows] += now[0:rows]
-
-    put(2 * rows, acc[...])
-    multiply(2 * rows, 0, mid)
+        multiply(rows, 0, 0, after_layer(0, 1))
+        multiply(rows, 0, 1, after_layer(rows, 0))
+
+    put(0, 2 * rows, acc[...])
+    multiply(2 * rows, 0, 0, store(mid, 2 * rows))
     land_ra[me] = acc[rows:2 * rows] * decays - mid[0:rows]
     land_ta[me] = acc[0:rows] * decays - mid[rows:2 * rows]
 
@@ -195,55 +225,58 @@
     g_rb.relay()
     g_ta.start()
     g_rb.finish()
-    put(rows, land_ta[me])
-    multiply(rows, 2, now)
+    put(0, rows, land_ta[me])
+    multiply(rows, 2, 0, store(acc, rows))
     t_across.wait_recv()
-    now[rows:2 * rows] = t_other[...]
-    acc[...] = now[...]
-
-    def first_chain(_k):
-        put(2 * rows, now[...])
-        multiply(2 * rows, 1, mid)
-        put(2 * rows, mid[...])
-        multiply(2 * rows, 2, now)
-        acc[...] += now[...]
-
-    pl.loop(0, 2)(first_chain)
-    g_ta.relay()
-    pl.loop(2, TERMS - 1)(first_chain)
+    acc[rows:2 * rows] = t_other[...]
+    powers(2 * rows, 1, 2, 1, g_ta.relay)
     g_ta.finish()
-    put(2 * rows, acc[...])
-    multiply(2 * rows, 0, mid)
+    put(0, 2 * rows, acc[...])
+    multiply(2 * rows, 0, 0, store(mid, 2 * rows))
     out1[...] = land_ra[me] + mid[0:rows]
     out2[...] = mid[rows:2 * rows]
 
     beside = layer * 3 - 3
     other = 3 - layer
     to_last = 2 - layer // 3
-    h1_near = zcopy(out1, land_h1.at[me], 2, 2, beside)
+    parts = [pl.ds(0, half), pl.ds(half, half)]
+    h1_near = [
+        zcopy(out1.at[part], land_h1.at[me, part], sem, sem, beside)
+        for part, sem in zip(parts, (2, 7))
+    ]
     h2_across = zcopy(out1, land_h2.at[me], 3, 3, other)
     s_near = zcopy(out2, start1, 4, 4, beside)
     l_far = zcopy(out2, land_l.at[me], 5, 5, to_last)
     h2_on = zcopy(land_h2.at[me], land_h2.at[me], 6, 3, beside)
-    h1_in = zcopy(land_h1.at[me], land_h1.at[me], 2, 2, other)
+    h1_in = [
+        zcopy(land_h1.at[me, part], land_h1.at[me, part], sem, sem, other)
+        for part, sem in zip(parts, (2, 7))
+    ]
     h2_in = zcopy(land_h2.at[me], land_h2.at[me], 3, 3, other)
     s_in = zcopy(start1, start1, 4, 4, other)
     l_in = zcopy(land_l.at[me], land_l.at[me], 5, 5, other)
 
     @pl.when(inner)
     def _():
-        h1_near.start()
+        for copy in h1_near:
+            copy.start()
         h2_across.start()
         land_h1[me] = out1[...]
-        now[0:rows] = out2[...]
+        acc[0:rows] = out2[...]
 
     @pl.when(outer)
     def _():
         land_l[me] = out2[...]
-        h1_in.wait_recv()
+        h1_in[0].wait_recv()
+
+    g_h1.start((0,))
+
+    @pl.when(outer)
+    def _():
+        h1_in[1].wait_recv()
         l_far.start()
 
-    g_h1.start()
+    g_h1.start((1,))
     g_h1.relay()
     h2_in.wait_recv()
 
@@ -266,29 +299,18 @@
     @pl.when(outer)
     def _():
         s_in.wait_recv()
-        now[0:rows] = start1[...]
-
-    acc[0:rows] = now[0:rows]
-
-    def second_chain(_k):
-        put(rows, now[0:rows])
-        multiply(rows, 2, mid)
-        put(rows, mid[0:rows])
-        multiply(rows, 1, now)
-        acc[0:rows] += now[0:rows]
-
-    pl.loop(0, 3)(second_chain)
-    g_l.relay()
-    pl.loop(3, TERMS - 1)(second_chain)
-
-    @pl.when(outer)
-    def _():
-        put(rows, acc[0:rows])
-        multiply(rows, 2, acc)
+        acc[0:rows] = start1[...]
+
+    powers(rows, 2, 1, 2, g_l.relay)
+
+    @pl.when(outer)
+    def _():
+        put(0, rows, acc[0:rows])
+        multiply(rows, 2, 0, store(acc, rows))
 
     g_l.finish()
-    put(rows, acc[0:rows])
-    multiply(rows, 0, mid)
+    put(0, rows, acc[0:rows])
+    multiply(rows, 0, 0, store(mid, rows))
 
     @pl.when(inner)
     def _():
@@ -305,7 +327,7 @@
 
     @pl.when(inner)
     def _():
-        for copy in (h1_near, h2_across, s_near, h2_on):
+        for copy in (*h1_near, h2_across, s_near, h2_on):
             copy.wait_send()
 
     @pl.when(outer)
@@ -332,10 +354,10 @@
         in_specs=[pl.BlockSpec(memory_space=pltpu.VMEM)] * 3,
         out_specs=pl.BlockSpec(memory_space=pltpu.VMEM),
         scratch_shapes=[whole] * 7 + [factors] * 2
-        + [pltpu.VMEM((4 * rows, order), jnp.bfloat16)]
+        + [pltpu.VMEM((2, 4 * rows, order), jnp.bfloat16)]
         + [pair] * 3 + [one] * 4
         + [pltpu.SemaphoreType.DMA((7, 2, n))] * 2
-        + [pltpu.SemaphoreType.DMA((7,))] * 2,
+        + [pltpu.SemaphoreType.DMA((8,))] * 2,
         compiler_params=pltpu.CompilerParams(
             collective_id=0, has_side_effects=True, vmem_limit_bytes=58 * 2**20
         ),

time: 198 us -> 173 us (0.87)
  Pallas kernels: 191 us -> 165 us
    pallas_call x1, Pallas kernels: 191 us -> 165 us  [local(): pl.pallas_call(functools.partial(kernel, n, rows, order), out_shape=jax.S...]
where the time goes in v1:
time: 173 us; the launch traced here: 172 us
  Pallas kernels  165 us (95%)
  local copies, waits for them, and re-layouts  4.53 us (3%)
    pallas_call x1, Pallas kernels, local(): pl.pallas_call(functools.partial(kernel, n, rows, order), out_shape=jax.S...  165 us

profile of v1, /device:TPU:0, one launch (start us, length us, event | category | flops | bytes accessed | tf_op | source)
XLA Modules:
  0.0 172.0 jit_solution(18060427609753943533)
XLA Ops:
  1.3 0.8 multiply_exponential_fusion.decay_ref
  2.1 0.0 copy-start
  2.1 0.8 copy.5.own_decay_ref
  2.9 1.9 %dynamic-slice_bitcast_fusion.refl_ref = f32[128,1024]{1,0:T(8,128)} fusion(f32[32,128,1024]{2,1,0:T(8,128)} %param.4, s32[]{:T(128)S(6)} %select_n.9), kind=kLoop, calls=%fused_computation | loop fusion | bytes 1048580 | tf_op jit(solution)/shard_map/jit(dynamic_index_in_dim)/squeeze | solution.py:342
  4.7 0.0 copy-done
  4.7 165.4 %shard_map.46 = f32[1,128,1024]{2,1,0:T(8,128)} custom-call(f32[128,1024]{1,0:T(8,128)} %dynamic-slice_bitcast_fusion.refl_ref, f32[1,1024]{1,0:T(1,128)} %copy-done, f32[128,1]{1,0:T(8,128)} %copy.5.own_decay_ref), custom_call_target="tpu_custom_call" | custom-call | tf_op jit(solution)/shard_map/pallas_call | solution.py:351
  170.1 1.9 %copy.9 = f32[1,128,1024]{2,1,0:T(8,128)} copy(f32[1,128,1024]{2,1,0:T(8,128)} %shard_map.46) | data formatting | bytes 1048576
  (1 shorter events, 0.0 us)
Async XLA Ops:
  2.1 2.7 %copy-start = (f32[1,1024]{1,0:T(1,128)}, f32[1,1024]{1,0:T(1,128)S(1)}, u32[]{:S(2)}) copy-start(f32[1,1024]{1,0:T(1,128)S(1)} %multiply_exponential_fusion.decay_ref) | copy-start | bytes 12292
